TPU v7x, 512 devices: a whole 4x8x8 slice. The times are simulated.
512 devices in a mesh: region: 32 (over y, z_hi), member: 16 (over x, z_lo, core).
Axes of the slice: x: 4, y: 8, z: 8 (z_hi: 4, z_lo: 2; z = z_hi * 2 + z_lo), core: 2. Of those that a mesh axis runs over, the one named last changes fastest.
Arguments:
- ensemble: bfloat16 [256, 262144], P('member', 'region'), may hold values from -6 to 6
- reports: float32 [32, 1024], P('region'), may hold values from -6 to 6
- report_count: int32 [32], P('region'), may hold values from 128 to 1024, as said below
- report_cell: int32 [32, 1024], P('region'), may hold values from 0 to 262143, as said below
- report_weight: float32 [32, 64, 1024], P('region', 'member'), may hold values from 0.001 to 1
- blending: float32 [4, 262144], P(None, ('region', 'member')), may hold values from 0.02 to 1
Outputs:
- analysis: bfloat16 [262144, 256], P(('region', 'member'))
Inputs may be any that keep to these rules, and one draw needn't show every extreme that they name: `report_count`: the largest value 1024 is reached by some region in every draw. `report_cell`: every cell lies in the slot's own region, or in the first 128 cells of one of at most two other regions chosen for that region.
All inputs are finite; a program needn't handle non-finite values.
Results may differ from a plain program's by a relative error of at most 0.0055.
Values may be sent and summed in bfloat16 or wider, within the bound.
A program may use at most 64 MiB of HBM per device.

v0:
```python
import jax
import jax.numpy as jnp
from jax import lax
from jax.sharding import PartitionSpec as P

MARGIN = 128
SWEEPS = 4
highest = lax.Precision.HIGHEST


def extended(block, sides, width):
    for axis, dim in sides:
        count = lax.axis_size(axis)
        forward = [(i, i + 1) for i in range(count - 1)]
        backward = [(target, source) for source, target in forward]
        low = lax.ppermute(
            lax.slice_in_dim(block, block.shape[dim] - width, None, axis=dim), axis, forward
        )
        high = lax.ppermute(lax.slice_in_dim(block, 0, width, axis=dim), axis, backward)
        block = jnp.concatenate([low, block, high], axis=dim)
    return block


def shifted(block, axis, distance):
    devices = range(lax.axis_size(axis))
    route = [(i - distance, i) for i in devices if i - distance in devices]
    return lax.ppermute(block, axis, route)


def make_transform(products, forcing, members):
    identity = jnp.eye(members, dtype=jnp.float32)
    precision_mat = (members - 1.0) * identity[None] + products
    frobenius = jnp.sqrt(jnp.sum(precision_mat * precision_mat, axis=(1, 2)))
    current = precision_mat / frobenius[:, None, None]
    root_iter = jnp.broadcast_to(identity, current.shape)
    for iteration in range(SWEEPS):
        middle = 1.5 * identity[None] - 0.5 * jnp.einsum(
            "aij,ajk->aik", root_iter, current, precision=highest
        )
        current = jnp.einsum("aij,ajk->aik", current, middle, precision=highest)
        root_iter = jnp.einsum("aij,ajk->aik", middle, root_iter, precision=highest)
    inverse_root = root_iter / jnp.sqrt(frobenius)[:, None, None]
    inner_step = jnp.einsum("aij,aj->ai", inverse_root, forcing, precision=highest)
    mean_weights = jnp.einsum("aij,aj->ai", inverse_root, inner_step, precision=highest)
    return (mean_weights[:, :, None] + jnp.sqrt(members - 1.0) * inverse_root).astype(jnp.bfloat16)


def corner_layout(band_index, points_here, row_count):
    group_index = jnp.arange(4 * points_here, dtype=jnp.int32)
    upper_half = group_index // (2 * points_here)
    column_block = group_index // 2 % points_here
    right_half = group_index % 2
    row_base = jnp.clip(band_index - 1 + upper_half, 0, row_count - 2)
    col_base = jnp.clip(column_block - 1 + right_half, 0, points_here - 2)
    return (row_base, col_base)


def per_device(ensemble, reports, report_count, report_cell, report_weight, blending):
    local_members, cell_count = ensemble.shape
    groups = lax.axis_size("member")
    members = local_members * groups
    region = lax.axis_index("region")
    member = lax.axis_index("member")
    targets = report_cell[0]
    holder = targets // cell_count
    within = targets % cell_count
    is_local = holder == region
    local_values = jnp.take(ensemble, jnp.where(is_local, within, 0), axis=1).astype(jnp.float32)
    border = ensemble[:, :MARGIN]
    border_index = holder * MARGIN + jnp.minimum(within, MARGIN - 1)
    pieces = lax.all_gather(border, "region", axis=1, tiled=True)
    extent = pieces.shape[1]
    inside = (border_index >= 0) & (border_index < extent) & jnp.logical_not(is_local)
    picked = jnp.take(pieces, jnp.clip(border_index, 0, extent - 1), axis=1).astype(jnp.float32)
    remote = jnp.where(inside[None, :], picked, 0.0)
    at_reports = jnp.where(is_local[None, :], local_values, remote)
    report_mean = lax.psum(jnp.sum(at_reports, axis=0), "member") / members
    local_pert = (at_reports - report_mean[None, :]).astype(jnp.bfloat16)
    report_pert = lax.all_gather(local_pert, "member", axis=0, tiled=True)
    active = (jnp.arange(report_pert.shape[1]) < report_count[0]).astype(jnp.float32)
    weights = report_weight[0] * active[None, :]
    weighted = (report_pert[None, :, :] * weights[:, None, :]).astype(jnp.bfloat16)
    departure = (weights * (reports[0] - report_mean)[None, :]).astype(jnp.bfloat16)
    products = jnp.einsum("ako,jo->akj", weighted, report_pert, preferred_element_type=jnp.float32)
    forcing = jnp.einsum("ao,ko->ak", departure, report_pert, preferred_element_type=jnp.float32)
    transform = make_transform(products, forcing, members)
    points_here = transform.shape[0]
    groups_band = 4 * points_here
    slab_cells = cell_count // groups
    group_cells = slab_cells // groups_band
    mixing = blending / jnp.sum(blending, axis=0, keepdims=True)
    everyone = lax.all_gather(ensemble, "member", axis=0, tiled=True)
    region_mean = jnp.sum(everyone, axis=0, dtype=jnp.float32) / members
    anomaly = (everyone - region_mean[None, :]).astype(jnp.bfloat16)
    near_mix = extended(mixing, (("member", 1),), slab_cells)
    totals = []
    for offset_band in range(3):
        band_index = member - 1 + offset_band
        slab_start = jnp.clip(band_index, 0, groups - 1) * slab_cells
        slab_anomaly = lax.dynamic_slice_in_dim(anomaly, slab_start, slab_cells, 1)
        slab_anomaly = slab_anomaly.reshape(members, groups_band, group_cells)
        mix_part = near_mix[:, offset_band * slab_cells : (offset_band + 1) * slab_cells]
        mix_part = mix_part.reshape(4, groups_band, group_cells)
        row_base, col_base = corner_layout(band_index, points_here, groups)
        row_step = (member - row_base)[:, None]
        running = jnp.zeros((groups_band, group_cells, members), jnp.float32)
        for col_step in range(2):
            weight = jnp.where(
                row_step == 0,
                mix_part[col_step],
                jnp.where(row_step == 1, mix_part[2 + col_step], 0.0),
            )
            chosen = jnp.take(transform, col_base + col_step, axis=0)
            spread = jnp.einsum(
                "kgc,gkj->gcj", slab_anomaly, chosen, preferred_element_type=jnp.float32
            )
            running = running + weight[:, :, None] * spread
        totals.append(running.reshape(slab_cells, members))
    from_below = shifted(totals[2], "member", 1)
    from_above = shifted(totals[0].astype(jnp.bfloat16), "member", -1).astype(jnp.float32)
    blended = totals[1] + from_below + from_above
    cell_mean = lax.dynamic_slice_in_dim(region_mean, member * slab_cells, slab_cells, 0)
    return (cell_mean[:, None] + blended).astype(jnp.bfloat16)


def solution(mesh):
    return jax.shard_map(
        per_device,
        mesh=mesh,
        in_specs=(
            P("member", "region"),
            P("region", None),
            P("region"),
            P("region", None),
            P("region", "member", None),
            P(None, ("region", "member")),
        ),
        out_specs=P(("region", "member"), None),
        check_vma=False,
    )
```

profile of v0, /device:TPU:1, one launch (start us, length us, event | category | flops | bytes accessed | tf_op | source)
XLA Modules:
  0.0 213.5 jit_solution(11608834173221068432)
XLA Ops:
  8.0 8.8 %collective-permute-start = (f32[4,512]{1,0:T(4,128)S(1)}, f32[4,512]{1,0:T(4,128)S(1)}, u32[]{:S(2)}, u32[]{:S(2)}) collective-permute-start(f32[4,512]{1,0:T(4,128)S(1)} %broadcast_divide_fusion.3), channel_id=1, source_target_pairs={{1,0},{2,1},{3,2},{4,3},{5,4},{6,5},{7,6},{8,7},{9,8},{10,9},{11,1... | collective-permute-start | bytes 24584 | tf_op jit(solution)/shard_map/ppermute | solution.py:19
  16.8 1.9 collective-permute-start.2
  18.7 1.9 copy.15
  20.8 3.2 %gather_fusion = bf16[1024,16]{1,0:T(8,128)(2,1)S(1)} fusion(bf16[16,8192]{0,1:T(8,128)(2,1)S(1)} %copy.15, s32[1024]{0:T(1024)S(1)} %broadcast_clamp_fusion.1), kind=kCustom, calls=%fused_computation.2 | custom fusion | bytes 69632 | tf_op jit(solution)/shard_map/jit(_take)/gather | solution.py:68
  24.1 76.4 %all_gather.10 = bf16[16,4096]{0,1:T(8,128)(2,1)S(1)} all-gather(bf16[16,128]{0,1:T(8,128)(2,1)S(1)} %slice.74), channel_id=1, replica_groups=mesh['region'=32,'member'=16] {'region'}, dimensions={1}, use_global_device_ids=true | all-gather | bytes 135168 | tf_op jit(solution)/shard_map/all_gather | solution.py:71
  100.5 3.2 %gather_fusion.1 = bf16[1024,16]{1,0:T(8,128)(2,1)S(1)} fusion(bf16[16,4096]{0,1:T(8,128)(2,1)S(1)} %all_gather.10, s32[1024]{0:T(1024)S(1)} %broadcast_clamp_fusion), kind=kCustom, calls=%fused_computation.3 | custom fusion | bytes 69632 | tf_op jit(solution)/shard_map/jit(_take)/gather | solution.py:74
  103.9 41.0 %psum.7 = f32[1024]{0:T(1024)S(1)} all-reduce(f32[1024]{0:T(1024)S(1)} %fusion.21), channel_id=1, replica_groups=mesh['region'=32,'member'=16] {'member'}, use_global_device_ids=true, to_apply=%region_3.4 | all-reduce | flops 1024 | bytes 8192 | tf_op jit(solution)/shard_map/psum | solution.py:77
  145.6 19.1 %all_gather.11 = bf16[256,1024]{1,0:T(8,128)(2,1)S(1)} all-gather(bf16[16,1024]{1,0:T(8,128)(2,1)S(1)} %fusion.22), channel_id=1, replica_groups=mesh['region'=32,'member'=16] {'member'}, dimensions={0}, use_global_device_ids=true | all-gather | bytes 557056 | tf_op jit(solution)/shard_map/all_gather | solution.py:79
  165.1 0.9 multiply_reduce_fusion
  166.0 1.2 fusion.8
  167.2 1.1 fusion.14
  168.3 1.2 fusion.20
  169.5 1.2 fusion.7
  170.7 1.1 fusion.42
  171.9 1.1 fusion.43
  173.0 1.2 fusion.6
  174.2 1.1 fusion.44
  175.4 1.1 fusion.45
  176.5 1.4 fusion.5
  177.9 1.1 convolution_divide_fusion
  179.0 1.0 fusion.28
  180.0 1.0 fusion.26
  182.5 2.0 gather_fusion.2
  185.4 3.0 %convert_reduce_fusion = f32[8192]{0:T(1024)S(1)} fusion(bf16[256,8192]{1,0:T(8,128)(2,1)} %all-gather.2.cloned.1.call-done), kind=kLoop, calls=%fused_computation.5 | loop fusion | flops 4186112 | bytes 4227072 | tf_op jit(solution)/shard_map/reduce_sum | solution.py:93
  188.8 0.9 fusion
  190.5 1.1 copy-done.1
  191.6 1.3 multiply_add_fusion
  192.9 2.8 %collective-permute-start.1 = (f32[512,256]{1,0:T(8,128)}, f32[512,256]{1,0:T(8,128)S(1)}, u32[]{:S(2)}, u32[]{:S(2)}) collective-permute-start(f32[512,256]{1,0:T(8,128)} %bitcast.16), channel_id=1, source_target_pairs={{0,1},{1,2},{2,3},{3,4},{4,5},{5,6},{6,7},{7,8},{8,9},{9,10},{10,1... | collective-permute-start | bytes 1572872 | tf_op jit(solution)/shard_map/ppermute | solution.py:27
  196.6 1.1 copy-done.2
  198.2 1.9 collective-permute-start.3
  201.2 4.6 %collective-permute-done.3 = bf16[512,256]{1,0:T(8,128)(2,1)S(1)} collective-permute-done((bf16[512,256]{1,0:T(8,128)(2,1)S(1)}, bf16[512,256]{1,0:T(8,128)(2,1)S(1)}, u32[]{:S(2)}, u32[]{:S(2)}) %collective-permute-start.3) | collective-permute-done | bytes 262176 | tf_op jit(solution)/shard_map/ppermute | solution.py:27
  205.9 0.8 fusion.12
  (80 shorter events, 8.2 us)
Async XLA Ops:
  6.5 14.1 %copy-start.3 = (s32[1,1024]{1,0:T(1,128)S(1)}, s32[1,1024]{1,0:T(1,128)}, u32[]{:S(2)}) copy-start(s32[1,1024]{1,0:T(1,128)} %param.11) | copy-start | bytes 12292
  6.5 178.8 %all-gather.2.cloned.1.call-start = ((), (), s32[]{:S(2)}) async-start(), calls=%async_computation | async-start | bytes 4456448 | tf_op jit(solution)/shard_map/all_gather | solution.py:92
  8.0 176.6 %collective-permute-start = (f32[4,512]{1,0:T(4,128)S(1)}, f32[4,512]{1,0:T(4,128)S(1)}, u32[]{:S(2)}, u32[]{:S(2)}) collective-permute-start(f32[4,512]{1,0:T(4,128)S(1)} %broadcast_divide_fusion.3), channel_id=1, source_target_pairs={{1,0},{2,1},{3,2},{4,3},{5,4},{6,5},{7,6},{8,7},{9,8},{10,9},{11,1... | collective-permute-start | bytes 24584 | tf_op jit(solution)/shard_map/ppermute | solution.py:19
  16.8 168.1 %collective-permute-start.2 = (f32[4,512]{1,0:T(4,128)S(1)}, f32[4,512]{1,0:T(4,128)S(1)}, u32[]{:S(2)}, u32[]{:S(2)}) collective-permute-start(f32[4,512]{1,0:T(4,128)S(1)} %broadcast_divide_fusion.3), channel_id=1, source_target_pairs={{0,1},{1,2},{2,3},{3,4},{4,5},{5,6},{6,7},{7,8},{8,9},{9,10},{10,1... | collective-permute-start | bytes 24584 | tf_op jit(solution)/shard_map/ppermute | solution.py:16
  18.7 126.2 %copy-start.5 = (f32[1,1024]{1,0:T(1,128)S(1)}, f32[1,1024]{1,0:T(1,128)}, u32[]{:S(2)}) copy-start(f32[1,1024]{1,0:T(1,128)} %param.9) | copy-start | bytes 12292
  100.5 64.4 %copy-start.4 = (f32[1,4,1024]{2,1,0:T(4,128)S(1)}, f32[1,4,1024]{2,1,0:T(4,128)}, u32[]{:S(2)}) copy-start(f32[1,4,1024]{2,1,0:T(4,128)} %param.12) | copy-start | bytes 49156
  185.4 3.5 %copy-start = (bf16[256,8192]{1,0:T(8,128)(2,1)S(1)}, bf16[256,8192]{1,0:T(8,128)(2,1)}, u32[]{:S(2)}) copy-start(bf16[256,8192]{1,0:T(8,128)(2,1)} %all-gather.2.cloned.1.call-done) | copy-start | bytes 12582916
  190.0 1.6 copy-start.1
  192.9 12.9 %collective-permute-start.1 = (f32[512,256]{1,0:T(8,128)}, f32[512,256]{1,0:T(8,128)S(1)}, u32[]{:S(2)}, u32[]{:S(2)}) collective-permute-start(f32[512,256]{1,0:T(8,128)} %bitcast.16), channel_id=1, source_target_pairs={{0,1},{1,2},{2,3},{3,4},{4,5},{5,6},{6,7},{7,8},{8,9},{9,10},{10,1... | collective-permute-start | bytes 1572872 | tf_op jit(solution)/shard_map/ppermute | solution.py:27
  196.0 1.6 copy-start.2
  198.2 7.7 %collective-permute-start.3 = (bf16[512,256]{1,0:T(8,128)(2,1)S(1)}, bf16[512,256]{1,0:T(8,128)(2,1)S(1)}, u32[]{:S(2)}, u32[]{:S(2)}) collective-permute-start(bf16[512,256]{1,0:T(8,128)(2,1)S(1)} %bitcast.89), channel_id=1, source_target_pairs={{1,0},{2,1},{3,2},{4,3},{5,4},{6,5},{7,6},{8,7},{9,8},{10,9},{11,1... | collective-permute-start | bytes 786440 | tf_op jit(solution)/shard_map/ppermute | solution.py:27
Sparse Core Ops, SparseCore 0:
  18.8 47.7 all-gather.1
where the time goes:
time: 214 us
  blocking collectives  136 us (64%)
  matrix products  19.9 us (9%)
  local copies, waits for them, and re-layouts  15.4 us (7%)
  starting transfers between devices  15.4 us (7%)
  between operations  14.5 us (7%)
  other arithmetic  7.2 us (3%)
  waiting for transfers between devices  4.65 us (2%)
    all_gather x1, blocking collectives, per_device(): pieces = lax.all_gather(border, 'region', axis=1, tiled=True)  76.4 us
    psum x1, blocking collectives, per_device(): report_mean = lax.psum(jnp.sum(at_reports, axis=0), 'member') / members  41 us
    all_gather x1, blocking collectives, per_device(): report_pert = lax.all_gather(local_pert, 'member', axis=0, tiled=True)  19.1 us
    ppermute x1, starting transfers between devices, extended(): lax.ppermute(lax.slice_in_dim(block, 0, width, axis=dim), axis, backward)  8.78 us
    dot_general x4, matrix products, make_transform(): jnp.einsum('aij,ajk->aik', root_iter, current, precision=highest)  4.9 us
    ppermute x2, starting transfers between devices, shifted(): return lax.ppermute(block, axis, route)  4.74 us
    ppermute x2, waiting for transfers between devices, shifted(): return lax.ppermute(block, axis, route)  4.63 us
    dot_general x4, matrix products, make_transform(): root_iter = jnp.einsum('aij,ajk->aik', middle, root_iter, precision=highest)  4.53 us
  transfers between devices with their start and end apart: 5, of which 1 were waited for; matrix products, arithmetic and copies ran while one was open for 15% of the time, Pallas kernels for 0%

commit v1 on v0

--- a/solution.py
+++ b/solution.py
@@ -2,10 +2,15 @@
 import jax.numpy as jnp
 from jax import lax
 from jax.sharding import PartitionSpec as P
+from jax.lax import all_gather
 
 MARGIN = 128
 SWEEPS = 4
 highest = lax.Precision.HIGHEST
+
+
+def get_plate(a0):
+    return all_gather(a0, axis_name="member").sum(axis=0)
 
 
 def extended(block, sides, width):
@@ -74,7 +79,7 @@
     picked = jnp.take(pieces, jnp.clip(border_index, 0, extent - 1), axis=1).astype(jnp.float32)
     remote = jnp.where(inside[None, :], picked, 0.0)
     at_reports = jnp.where(is_local[None, :], local_values, remote)
-    report_mean = lax.psum(jnp.sum(at_reports, axis=0), "member") / members
+    report_mean = get_plate(jnp.sum(at_reports, axis=0)) / members
     local_pert = (at_reports - report_mean[None, :]).astype(jnp.bfloat16)
     report_pert = lax.all_gather(local_pert, "member", axis=0, tiled=True)
     active = (jnp.arange(report_pert.shape[1]) < report_count[0]).astype(jnp.float32)

time: 214 us -> 206 us (0.963)
  blocking collectives: 136 us -> 128 us
    psum x1 -> x0, blocking collectives: 41 us -> none  [per_device(): report_mean = lax.psum(jnp.sum(at_reports, axis=0), 'member') / members]
    all_gather x0 -> x1, blocking collectives: none -> 33.1 us  [get_plate(): return all_gather(a0, axis_name='member').sum(axis=0)]
where the time goes in v1:
time: 206 us; the launch traced here: 205 us
  blocking collectives  128 us (62%)
  matrix products  19.9 us (10%)
  starting transfers between devices  15.7 us (8%)
  local copies, waits for them, and re-layouts  15.4 us (7%)
  between operations  14.6 us (7%)
  other arithmetic  7.23 us (4%)
  waiting for transfers between devices  4.65 us (2%)
    all_gather x1, blocking collectives, per_device(): pieces = lax.all_gather(border, 'region', axis=1, tiled=True)  76.3 us
    all_gather x1, blocking collectives, get_plate(): return all_gather(a0, axis_name='member').sum(axis=0)  33.1 us
    all_gather x1, blocking collectives, per_device(): report_pert = lax.all_gather(local_pert, 'member', axis=0, tiled=True)  18.6 us
    ppermute x1, starting transfers between devices, extended(): lax.ppermute(lax.slice_in_dim(block, 0, width, axis=dim), axis, backward)  8.78 us
    ppermute x2, starting transfers between devices, shifted(): return lax.ppermute(block, axis, route)  5.01 us
    dot_general x4, matrix products, make_transform(): jnp.einsum('aij,ajk->aik', root_iter, current, precision=highest)  4.91 us
    ppermute x2, waiting for transfers between devices, shifted(): return lax.ppermute(block, axis, route)  4.63 us
    dot_general x4, matrix products, make_transform(): root_iter = jnp.einsum('aij,ajk->aik', middle, root_iter, precision=highest)  4.53 us
  transfers between devices with their start and end apart: 5, of which 1 were waited for; matrix products, arithmetic and copies ran while one was open for 15% of the time, Pallas kernels for 0%

profile of v1, /device:TPU:1, one launch (start us, length us, event | category | flops | bytes accessed | tf_op | source)
XLA Modules:
  0.0 205.4 jit_solution(6713759882962123731)
XLA Ops:
  8.0 8.8 %collective-permute-start = (f32[4,512]{1,0:T(4,128)S(1)}, f32[4,512]{1,0:T(4,128)S(1)}, u32[]{:S(2)}, u32[]{:S(2)}) collective-permute-start(f32[4,512]{1,0:T(4,128)S(1)} %broadcast_divide_fusion.3), channel_id=1, source_target_pairs={{1,0},{2,1},{3,2},{4,3},{5,4},{6,5},{7,6},{8,7},{9,8},{10,9},{11,1... | collective-permute-start | bytes 24584 | tf_op jit(solution)/shard_map/ppermute | solution.py:24
  16.8 1.9 collective-permute-start.2
  18.7 1.9 copy.29
  20.8 3.2 %gather_fusion = bf16[1024,16]{1,0:T(8,128)(2,1)S(1)} fusion(bf16[16,8192]{0,1:T(8,128)(2,1)S(1)} %copy.29, s32[1024]{0:T(1024)S(1)} %broadcast_clamp_fusion.1), kind=kCustom, calls=%fused_computation.2 | custom fusion | bytes 69632 | tf_op jit(solution)/shard_map/jit(_take)/gather | solution.py:73
  24.1 76.3 %all_gather.16 = bf16[16,4096]{0,1:T(8,128)(2,1)S(1)} all-gather(bf16[16,128]{0,1:T(8,128)(2,1)S(1)} %slice.74), channel_id=1, replica_groups=mesh['region'=32,'member'=16] {'region'}, dimensions={1}, use_global_device_ids=true | all-gather | bytes 135168 | tf_op jit(solution)/shard_map/all_gather | solution.py:76
  100.4 3.2 %gather_fusion.1 = bf16[1024,16]{1,0:T(8,128)(2,1)S(1)} fusion(bf16[16,4096]{0,1:T(8,128)(2,1)S(1)} %all_gather.16, s32[1024]{0:T(1024)S(1)} %broadcast_clamp_fusion), kind=kCustom, calls=%fused_computation.3 | custom fusion | bytes 69632 | tf_op jit(solution)/shard_map/jit(_take)/gather | solution.py:79
  103.8 33.1 %all-gather = f32[16384]{0:T(1024)S(1)} all-gather(f32[1024]{0:T(1024)S(1)} %fusion.21), channel_id=2, replica_groups=mesh['region'=32,'member'=16] {'member'}, dimensions={0}, use_global_device_ids=true | all-gather | bytes 69632 | tf_op jit(solution)/shard_map/all_gather | solution.py:13
  137.7 18.6 %all_gather.19 = bf16[256,1024]{1,0:T(8,128)(2,1)S(1)} all-gather(bf16[16,1024]{1,0:T(8,128)(2,1)S(1)} %fusion.22), channel_id=1, replica_groups=mesh['region'=32,'member'=16] {'member'}, dimensions={0}, use_global_device_ids=true | all-gather | bytes 557056 | tf_op jit(solution)/shard_map/all_gather | solution.py:84
  156.8 0.9 multiply_reduce_fusion
  157.7 1.2 fusion.8
  158.8 1.1 fusion.14
  159.9 1.2 fusion.20
  161.1 1.2 fusion.7
  162.3 1.1 fusion.41
  163.5 1.1 fusion.42
  164.6 1.2 fusion.6
  165.8 1.1 fusion.43
  167.0 1.1 fusion.44
  168.2 1.4 fusion.5
  169.5 1.1 convolution_divide_fusion
  170.7 1.0 fusion.28
  171.7 1.0 fusion.26
  174.1 2.0 gather_fusion.2
  177.0 3.0 %convert_reduce_fusion = f32[8192]{0:T(1024)S(1)} fusion(bf16[256,8192]{1,0:T(8,128)(2,1)} %all-gather.3.cloned.1.call-done), kind=kLoop, calls=%fused_computation.5 | loop fusion | flops 4186112 | bytes 4227072 | tf_op jit(solution)/shard_map/reduce_sum | solution.py:98
  180.5 0.9 fusion
  182.2 1.1 copy-done.1
  183.2 1.3 multiply_add_fusion
  184.6 3.1 %collective-permute-start.1 = (f32[512,256]{1,0:T(8,128)}, f32[512,256]{1,0:T(8,128)S(1)}, u32[]{:S(2)}, u32[]{:S(2)}) collective-permute-start(f32[512,256]{1,0:T(8,128)} %bitcast.17), channel_id=1, source_target_pairs={{0,1},{1,2},{2,3},{3,4},{4,5},{5,6},{6,7},{7,8},{8,9},{9,10},{10,1... | collective-permute-start | bytes 1572872 | tf_op jit(solution)/shard_map/ppermute | solution.py:32
  188.5 1.1 copy-done.2
  190.1 1.9 collective-permute-start.3
  193.1 4.6 %collective-permute-done.3 = bf16[512,256]{1,0:T(8,128)(2,1)S(1)} collective-permute-done((bf16[512,256]{1,0:T(8,128)(2,1)S(1)}, bf16[512,256]{1,0:T(8,128)(2,1)S(1)}, u32[]{:S(2)}, u32[]{:S(2)}) %collective-permute-start.3) | collective-permute-done | bytes 262176 | tf_op jit(solution)/shard_map/ppermute | solution.py:32
  197.8 0.8 fusion.12
  (83 shorter events, 8.2 us)
Async XLA Ops:
  6.5 14.1 %copy-start.3 = (s32[1,1024]{1,0:T(1,128)S(1)}, s32[1,1024]{1,0:T(1,128)}, u32[]{:S(2)}) copy-start(s32[1,1024]{1,0:T(1,128)} %param.11) | copy-start | bytes 12292
  6.5 170.5 %all-gather.3.cloned.1.call-start = ((), (), s32[]{:S(2)}) async-start(), calls=%async_computation | async-start | bytes 4456448 | tf_op jit(solution)/shard_map/all_gather | solution.py:97
  8.0 168.2 %collective-permute-start = (f32[4,512]{1,0:T(4,128)S(1)}, f32[4,512]{1,0:T(4,128)S(1)}, u32[]{:S(2)}, u32[]{:S(2)}) collective-permute-start(f32[4,512]{1,0:T(4,128)S(1)} %broadcast_divide_fusion.3), channel_id=1, source_target_pairs={{1,0},{2,1},{3,2},{4,3},{5,4},{6,5},{7,6},{8,7},{9,8},{10,9},{11,1... | collective-permute-start | bytes 24584 | tf_op jit(solution)/shard_map/ppermute | solution.py:24
  16.8 159.8 %collective-permute-start.2 = (f32[4,512]{1,0:T(4,128)S(1)}, f32[4,512]{1,0:T(4,128)S(1)}, u32[]{:S(2)}, u32[]{:S(2)}) collective-permute-start(f32[4,512]{1,0:T(4,128)S(1)} %broadcast_divide_fusion.3), channel_id=1, source_target_pairs={{0,1},{1,2},{2,3},{3,4},{4,5},{5,6},{6,7},{7,8},{8,9},{9,10},{10,1... | collective-permute-start | bytes 24584 | tf_op jit(solution)/shard_map/ppermute | solution.py:21
  24.1 132.3 %copy-start.5 = (f32[1,1024]{1,0:T(1,128)S(1)}, f32[1,1024]{1,0:T(1,128)}, u32[]{:S(2)}) copy-start(f32[1,1024]{1,0:T(1,128)} %param.9) | copy-start | bytes 12292
  100.4 56.1 %copy-start.4 = (f32[1,4,1024]{2,1,0:T(4,128)S(1)}, f32[1,4,1024]{2,1,0:T(4,128)}, u32[]{:S(2)}) copy-start(f32[1,4,1024]{2,1,0:T(4,128)} %param.12) | copy-start | bytes 49156
  177.0 3.5 %copy-start = (bf16[256,8192]{1,0:T(8,128)(2,1)S(1)}, bf16[256,8192]{1,0:T(8,128)(2,1)}, u32[]{:S(2)}) copy-start(bf16[256,8192]{1,0:T(8,128)(2,1)} %all-gather.3.cloned.1.call-done) | copy-start | bytes 12582916
  181.6 1.6 copy-start.1
  184.6 13.2 %collective-permute-start.1 = (f32[512,256]{1,0:T(8,128)}, f32[512,256]{1,0:T(8,128)S(1)}, u32[]{:S(2)}, u32[]{:S(2)}) collective-permute-start(f32[512,256]{1,0:T(8,128)} %bitcast.17), channel_id=1, source_target_pairs={{0,1},{1,2},{2,3},{3,4},{4,5},{5,6},{6,7},{7,8},{8,9},{9,10},{10,1... | collective-permute-start | bytes 1572872 | tf_op jit(solution)/shard_map/ppermute | solution.py:32
  187.9 1.6 copy-start.2
  190.1 7.7 %collective-permute-start.3 = (bf16[512,256]{1,0:T(8,128)(2,1)S(1)}, bf16[512,256]{1,0:T(8,128)(2,1)S(1)}, u32[]{:S(2)}, u32[]{:S(2)}) collective-permute-start(bf16[512,256]{1,0:T(8,128)(2,1)S(1)} %bitcast.91), channel_id=1, source_target_pairs={{1,0},{2,1},{3,2},{4,3},{5,4},{6,5},{7,6},{8,7},{9,8},{10,9},{11,1... | collective-permute-start | bytes 786440 | tf_op jit(solution)/shard_map/ppermute | solution.py:32
Sparse Core Ops, SparseCore 0:
  18.8 47.7 all-gather.2
